TPU v7x, 32 devices: a whole 2x2x4 slice. The times are simulated.
32 devices in a mesh: tm: 4 (over x, core), batch: 8 (over z, y).
Axes of the slice: x: 2, y: 2, z: 4, core: 2. Of those that a mesh axis runs over, the one named last changes fastest.
Arguments:
- inputs: bfloat16 [1536, 24, 100], P(('tm', 'batch')), may hold values from -6 to 6
- lengths: int32 [1536], P(('tm', 'batch')), may hold values from 5 to 21, as said below
- w_rec: bfloat16 [400, 400], P(None, 'tm'), may hold values from -0.3125 to 0.3125
- w_in: bfloat16 [100, 400], P(None, 'tm'), may hold values from -0.625 to 0.625
- rec_bias: float32 [400], replicated, may hold values from -3 to 3
- norm_gain: float32 [400], replicated, may hold values from 0.5 to 1.5
- norm_shift: float32 [400], replicated, may hold values from -2 to 2
- cotangent: bfloat16 [1536, 24, 400], P(('tm', 'batch')), may hold values from -6 to 6
Outputs:
- hidden: bfloat16 [1536, 24, 400], P(('tm', 'batch'))
- grad_inputs: float32 [1536, 24, 100], P(('tm', 'batch'))
- grad_w_rec: float32 [400, 400], P(None, 'tm')
- grad_w_in: float32 [100, 400], P(None, 'tm')
- grad_rec_bias: float32 [400], P('tm')
- grad_norm_gain: float32 [400], P('tm')
- grad_norm_shift: float32 [400], P('tm')
Inputs may be any that keep to these rules, and one draw needn't show every extreme that they name: Steps t < lengths[b] are valid. In each aligned block of 48 sequences one has length 21 and the next (cyclically) length 5.
All inputs are finite; a program needn't handle non-finite values.
Results may differ from a plain program's by a relative error of at most 0.0053.
Values may be sent and summed in bfloat16 or wider, within the bound.
A program may use at most 256 MiB of HBM per device.

v0:
```python
import jax
import jax.numpy as jnp
from jax import lax
from jax.sharding import PartitionSpec as P

MICRO = 2


DECAY_RATE = 0.95
FAST_RATE = 0.5
NORM_EPS = 1e-05
EXACT = lax.Precision.HIGHEST


def norm_silu(mixed_pre, norm_gain, norm_shift):
    centre_mean = jnp.mean(mixed_pre, -1, keepdims=True)
    centred = mixed_pre - centre_mean
    spread = jnp.mean(centred * centred, -1, keepdims=True)
    return jax.nn.silu(centred * lax.rsqrt(spread + NORM_EPS) * norm_gain + norm_shift)


def silu_slope(values):
    sigmoid_val = jax.nn.sigmoid(values)
    return sigmoid_val * (1.0 + values * (1.0 - sigmoid_val))


def run_block(inputs, in_seq, state_h, weights):
    w_rec, w_in, rec_bias, norm_gain, norm_shift = weights
    count_steps = inputs.shape[1]
    current = state_h
    past_list, pre_list, first_list, mixed_list, out_list = ([], [], [], [], [])
    for j in range(count_steps):
        past_list.append(current)
        earlier = jnp.stack(past_list, 1)
        pre_act = (
            jnp.dot(current.astype(jnp.bfloat16), w_rec, preferred_element_type=jnp.float32)
            + jnp.dot(inputs[:, j], w_in, preferred_element_type=jnp.float32)
            + rec_bias
        )
        first_act = jax.nn.silu(pre_act)
        decays = jnp.power(DECAY_RATE, jnp.arange(j, -1, -1).astype(jnp.float32))
        coef_row = jnp.einsum("bih,bh->bi", earlier, first_act, precision=EXACT) * decays
        fast_term = FAST_RATE * jnp.einsum("bi,bih->bh", coef_row, earlier, precision=EXACT)
        mixed_pre = pre_act + fast_term
        current = jnp.where(
            in_seq[:, j : j + 1], norm_silu(mixed_pre, norm_gain, norm_shift), current
        )
        pre_list.append(pre_act)
        first_list.append(first_act)
        mixed_list.append(mixed_pre)
        out_list.append(current)
    past_hidden = jnp.stack(past_list, 1)
    saved_acts = (
        past_hidden,
        jnp.stack(pre_list, 1),
        jnp.stack(first_list, 1),
        jnp.stack(mixed_list, 1),
    )
    return (current, jnp.stack(out_list, 1), saved_acts)


def back_block(inputs, in_seq, saved_acts, grad_h, upstream, weights):
    w_rec, w_in, rec_bias, norm_gain, norm_shift = weights
    past_hidden, pre_acts, first_acts, mixed_acts = saved_acts
    count_steps = inputs.shape[1]
    hidden_width = w_rec.shape[0]
    rec_sum = jnp.zeros((hidden_width, hidden_width), jnp.float32)
    in_sum = jnp.zeros(w_in.shape, jnp.float32)
    bias_sum = jnp.zeros((hidden_width,), jnp.float32)
    gain_sum = jnp.zeros((hidden_width,), jnp.float32)
    shift_sum = jnp.zeros((hidden_width,), jnp.float32)
    slope_list = [None] * count_steps
    input_grads = [None] * count_steps
    grad_now = grad_h
    for j in reversed(range(count_steps)):
        keep_now = in_seq[:, j : j + 1]
        total_grad = grad_now + upstream[:, j]
        grad_norm_out = jnp.where(keep_now, total_grad, 0.0)
        passed_on = jnp.where(keep_now, 0.0, total_grad)
        _, pull_back = jax.vjp(norm_silu, mixed_acts[:, j], norm_gain, norm_shift)
        d_mix, d_gain, d_shift = pull_back(grad_norm_out)
        earlier = past_hidden[:, : j + 1]
        decays = jnp.power(DECAY_RATE, jnp.arange(j, -1, -1).astype(jnp.float32))
        coef_row = jnp.einsum("bih,bh->bi", earlier, d_mix, precision=EXACT) * decays
        d_first = FAST_RATE * jnp.einsum("bi,bih->bh", coef_row, earlier, precision=EXACT)
        d_pre = (d_mix + d_first * silu_slope(pre_acts[:, j])).astype(jnp.bfloat16)
        p_now = past_hidden[:, j]
        rec_sum = rec_sum + jnp.dot(
            p_now.astype(jnp.bfloat16).T, d_pre, preferred_element_type=jnp.float32
        )
        in_sum = in_sum + jnp.dot(inputs[:, j].T, d_pre, preferred_element_type=jnp.float32)
        bias_sum = bias_sum + jnp.sum(d_pre.astype(jnp.float32), 0)
        gain_sum = gain_sum + d_gain
        shift_sum = shift_sum + d_shift
        input_grads[j] = jnp.dot(d_pre, w_in.T, preferred_element_type=jnp.float32)
        slope_list[j] = d_mix
        later_mix = jnp.stack(slope_list[j:], 1)
        later_first = first_acts[:, j:]
        ahead = jnp.power(DECAY_RATE, jnp.arange(count_steps - j).astype(jnp.float32))
        first_coef = jnp.einsum("bih,bh->bi", later_first, p_now, precision=EXACT) * ahead
        mix_coef = jnp.einsum("bih,bh->bi", later_mix, p_now, precision=EXACT) * ahead
        sym_term = jnp.einsum("bi,bih->bh", first_coef, later_mix, precision=EXACT) + jnp.einsum(
            "bi,bih->bh", mix_coef, later_first, precision=EXACT
        )
        from_rec = jnp.dot(d_pre, w_rec.T, preferred_element_type=jnp.float32)
        grad_now = passed_on + jnp.where(keep_now, from_rec + FAST_RATE * sym_term, 0.0)
    return ((rec_sum, in_sum, bias_sum, gain_sum, shift_sum), jnp.stack(input_grads, 1))


def per_device(inputs, lengths, w_rec, w_in, rec_bias, norm_gain, norm_shift, cotangent):
    tm_rank = lax.axis_index("tm")
    local_rows, seq_steps, embed_width = inputs.shape
    share_cols = w_rec.shape[1]
    rec_full, in_full = (
        lax.all_gather(w_rec, "tm", axis=1, tiled=True),
        lax.all_gather(w_in, "tm", axis=1, tiled=True),
    )
    hidden_width = rec_full.shape[0]
    weights = (rec_full, in_full, rec_bias, norm_gain, norm_shift)
    upstream = cotangent.astype(jnp.float32)
    step_ids = jnp.arange(seq_steps, dtype=jnp.int32)
    in_seq = step_ids[None, :] < lengths[:, None]
    micro_rows = local_rows // MICRO
    sums = (
        jnp.zeros((hidden_width, hidden_width), jnp.float32),
        jnp.zeros((embed_width, hidden_width), jnp.float32),
        jnp.zeros((hidden_width,), jnp.float32),
        jnp.zeros((hidden_width,), jnp.float32),
        jnp.zeros((hidden_width,), jnp.float32),
    )
    hidden_parts, grad_parts = ([], [])
    for micro_no in range(MICRO):
        lower = micro_no * micro_rows
        upper = lower + micro_rows
        part_in = inputs[lower:upper]
        part_seq = in_seq[lower:upper]
        blank_h = jnp.zeros((micro_rows, hidden_width), jnp.float32)
        forward_out = run_block(part_in, part_seq, blank_h, weights)
        part_sums, part_grad = back_block(
            part_in, part_seq, forward_out[2], blank_h, upstream[lower:upper], weights
        )
        sums = tuple((total + piece for total, piece in zip(sums, part_sums)))
        hidden_parts.append(forward_out[1])
        grad_parts.append(part_grad)
    hidden = jnp.concatenate(hidden_parts, 0)
    grad_x = jnp.concatenate(grad_parts, 0)
    whole = lax.psum((sums[0], sums[1], sums[2], sums[3], sums[4]), ("tm", "batch"))
    first_col = tm_rank * share_cols
    totals = (
        lax.dynamic_slice_in_dim(whole[0], first_col, share_cols, 1),
        lax.dynamic_slice_in_dim(whole[1], first_col, share_cols, 1),
        lax.dynamic_slice_in_dim(whole[2], first_col, share_cols, 0),
        lax.dynamic_slice_in_dim(whole[3], first_col, share_cols, 0),
        lax.dynamic_slice_in_dim(whole[4], first_col, share_cols, 0),
    )
    return (
        hidden.astype(jnp.bfloat16),
        grad_x,
        totals[0],
        totals[1],
        totals[2],
        totals[3],
        totals[4],
    )


def solution(mesh):
    return jax.shard_map(
        per_device,
        mesh=mesh,
        in_specs=(
            P(("tm", "batch"), None, None),
            P(("tm", "batch")),
            P(None, "tm"),
            P(None, "tm"),
            P(),
            P(),
            P(),
            P(("tm", "batch"), None, None),
        ),
        out_specs=(
            P(("tm", "batch"), None, None),
            P(("tm", "batch"), None, None),
            P(None, "tm"),
            P(None, "tm"),
            P("tm"),
            P("tm"),
            P("tm"),
        ),
        check_vma=False,
    )
```

profile of v0, /device:TPU:0, one launch (start us, length us, event | category | flops | bytes accessed | tf_op | source)
XLA Modules:
  0.0 880.6 jit_solution(15626808526295222519)
XLA Ops:
  7.2 2.7 fusion.1998
  9.9 2.3 fusion.1999
  51.7 6.3 all-gather.1
  58.1 7.2 all-gather
  142.0 2.2 fusion.79
  154.0 1.9 fusion.428
  159.1 1.9 fusion.460
  231.8 1.9 fusion.420
  237.7 1.9 fusion.452
  244.8 1.9 fusion.484
  246.8 1.9 fusion.492
  258.0 1.9 fusion.480
  260.3 1.9 fusion.488
  267.9 1.9 fusion.448
  270.1 1.9 fusion.456
  283.5 1.9 fusion.416
  285.6 1.9 fusion.424
  301.3 1.9 fusion.139
  356.5 2.4 fusion.788
  375.1 2.2 fusion.804
  586.8 1.9 fusion.105
  604.3 2.0 fusion.113
  630.4 1.9 fusion.151
  654.3 1.9 fusion.183
  656.2 1.9 fusion.185
  658.1 2.1 fusion.191
  673.0 1.9 fusion.218
  674.9 2.3 fusion.224
  677.2 1.9 fusion.216
  688.5 1.9 fusion.210
  758.7 40.8 %all-reduce.2 = (f32[400]{0:T(512)S(1)}, f32[400]{0:T(512)S(1)}, f32[400]{0:T(512)S(1)}) all-reduce(f32[400]{0:T(512)S(1)} %add_add_fusion.50, f32[400]{0:T(512)S(1)} %add_add_fusion.49, f32[400]{0:T(512)S(1)} %add_add_fusion.48), channel_id=1, replica_groups=mesh['tm'=4,'batch'=8] {'tm','batch'}, use_global_device_ids=true, to_apply=%region_242.243 | all-reduce | flops 1200 | bytes 9600 | tf_op jit(solution)/shard_map/psum | solution.py:147
  804.3 65.9 %all-reduce.6.cloned.1.call-done = (f32[400,400]{1,0:T(8,128)}, f32[100,400]{0,1:T(8,128)}) async-done(((f32[400,400]{1,0:T(8,128)}, f32[100,400]{0,1:T(8,128)}), (f32[400,400]{1,0:T(8,128)}, f32[100,400]{0,1:T(8,128)})) %all-reduce.6.cloned.1.call-update) | async-done | bytes 800016 | tf_op jit(solution)/shard_map/psum | solution.py:147
  (4055 shorter events, 670.0 us)
Async XLA Ops:
  7.2 863.0 %all-reduce.6.cloned.1.call-start = ((), (), s32[]{:S(2)}) async-start(), calls=%async_computation | async-start | bytes 2048000 | tf_op jit(solution)/shard_map/psum | solution.py:147
  71.6 649.8 %copy-start.39 = (f32[24,400]{1,0:T(8,128)}, f32[24,400]{1,0:T(8,128)S(1)}, u32[]{:S(2)}) copy-start(f32[24,400]{1,0:T(8,128)S(1)} %get-tuple-element.1798) | copy-start | bytes 115204
  71.6 663.1 %copy-start.37 = (f32[24,400]{1,0:T(8,128)}, f32[24,400]{1,0:T(8,128)S(1)}, u32[]{:S(2)}) copy-start(f32[24,400]{1,0:T(8,128)S(1)} %get-tuple-element.466) | copy-start | bytes 115204
  77.0 644.1 %copy-start.43 = (f32[24,400]{1,0:T(8,128)}, f32[24,400]{1,0:T(8,128)S(1)}, u32[]{:S(2)}) copy-start(f32[24,400]{1,0:T(8,128)S(1)} %get-tuple-element.556) | copy-start | bytes 115204
  77.0 656.7 %copy-start.41 = (f32[24,400]{1,0:T(8,128)}, f32[24,400]{1,0:T(8,128)S(1)}, u32[]{:S(2)}) copy-start(f32[24,400]{1,0:T(8,128)S(1)} %get-tuple-element.1701) | copy-start | bytes 115204
  81.9 638.8 %copy-start.49 = (f32[24,400]{1,0:T(8,128)}, f32[24,400]{1,0:T(8,128)S(1)}, u32[]{:S(2)}) copy-start(f32[24,400]{1,0:T(8,128)S(1)} %get-tuple-element.554) | copy-start | bytes 115204
  264.3 420.4 %copy-start.435 = (bf16[24,400]{1,0:T(8,128)(2,1)}, bf16[24,400]{1,0:T(8,128)(2,1)S(1)}, u32[]{:S(2)}) copy-start(bf16[24,400]{1,0:T(8,128)(2,1)S(1)} %get-tuple-element.656) | copy-start | bytes 57604
  266.5 418.0 %copy-start.433 = (bf16[24,400]{1,0:T(8,128)(2,1)}, bf16[24,400]{1,0:T(8,128)(2,1)S(1)}, u32[]{:S(2)}) copy-start(bf16[24,400]{1,0:T(8,128)(2,1)S(1)} %get-tuple-element.658) | copy-start | bytes 57604
  274.2 447.5 %copy-start.437 = (bf16[24,400]{1,0:T(8,128)(2,1)}, bf16[24,400]{1,0:T(8,128)(2,1)S(1)}, u32[]{:S(2)}) copy-start(bf16[24,400]{1,0:T(8,128)(2,1)S(1)} %get-tuple-element.182) | copy-start | bytes 57604
  289.6 432.4 %copy-start.439 = (bf16[24,400]{1,0:T(8,128)(2,1)}, bf16[24,400]{1,0:T(8,128)(2,1)S(1)}, u32[]{:S(2)}) copy-start(bf16[24,400]{1,0:T(8,128)(2,1)S(1)} %get-tuple-element.186) | copy-start | bytes 57604
  297.8 417.3 %copy-start.383 = (bf16[24,400]{1,0:T(8,128)(2,1)}, bf16[24,400]{1,0:T(8,128)(2,1)S(1)}, u32[]{:S(2)}) copy-start(bf16[24,400]{1,0:T(8,128)(2,1)S(1)} %get-tuple-element.234) | copy-start | bytes 57604
  306.1 416.2 %copy-start.441 = (bf16[24,400]{1,0:T(8,128)(2,1)}, bf16[24,400]{1,0:T(8,128)(2,1)S(1)}, u32[]{:S(2)}) copy-start(bf16[24,400]{1,0:T(8,128)(2,1)S(1)} %get-tuple-element.188) | copy-start | bytes 57604
  314.7 400.7 %copy-start.385 = (bf16[24,400]{1,0:T(8,128)(2,1)}, bf16[24,400]{1,0:T(8,128)(2,1)S(1)}, u32[]{:S(2)}) copy-start(bf16[24,400]{1,0:T(8,128)(2,1)S(1)} %get-tuple-element.236) | copy-start | bytes 57604
  322.2 400.4 %copy-start.443 = (bf16[24,400]{1,0:T(8,128)(2,1)}, bf16[24,400]{1,0:T(8,128)(2,1)S(1)}, u32[]{:S(2)}) copy-start(bf16[24,400]{1,0:T(8,128)(2,1)S(1)} %get-tuple-element.190) | copy-start | bytes 57604
  330.8 384.9 %copy-start.387 = (bf16[24,400]{1,0:T(8,128)(2,1)}, bf16[24,400]{1,0:T(8,128)(2,1)S(1)}, u32[]{:S(2)}) copy-start(bf16[24,400]{1,0:T(8,128)(2,1)S(1)} %get-tuple-element.238) | copy-start | bytes 57604
  338.2 384.8 %copy-start.445 = (bf16[24,400]{1,0:T(8,128)(2,1)}, bf16[24,400]{1,0:T(8,128)(2,1)S(1)}, u32[]{:S(2)}) copy-start(bf16[24,400]{1,0:T(8,128)(2,1)S(1)} %get-tuple-element.192) | copy-start | bytes 57604
  348.1 368.0 %copy-start.389 = (bf16[24,400]{1,0:T(8,128)(2,1)}, bf16[24,400]{1,0:T(8,128)(2,1)S(1)}, u32[]{:S(2)}) copy-start(bf16[24,400]{1,0:T(8,128)(2,1)S(1)} %get-tuple-element.240) | copy-start | bytes 57604
  355.2 368.0 %copy-start.447 = (bf16[24,400]{1,0:T(8,128)(2,1)}, bf16[24,400]{1,0:T(8,128)(2,1)S(1)}, u32[]{:S(2)}) copy-start(bf16[24,400]{1,0:T(8,128)(2,1)S(1)} %get-tuple-element.194) | copy-start | bytes 57604
  366.7 349.6 %copy-start.391 = (bf16[24,400]{1,0:T(8,128)(2,1)}, bf16[24,400]{1,0:T(8,128)(2,1)S(1)}, u32[]{:S(2)}) copy-start(bf16[24,400]{1,0:T(8,128)(2,1)S(1)} %get-tuple-element.242) | copy-start | bytes 57604
  373.8 349.8 %copy-start.449 = (bf16[24,400]{1,0:T(8,128)(2,1)}, bf16[24,400]{1,0:T(8,128)(2,1)S(1)}, u32[]{:S(2)}) copy-start(bf16[24,400]{1,0:T(8,128)(2,1)S(1)} %get-tuple-element.196) | copy-start | bytes 57604
  385.3 331.4 %copy-start.393 = (bf16[24,400]{1,0:T(8,128)(2,1)}, bf16[24,400]{1,0:T(8,128)(2,1)S(1)}, u32[]{:S(2)}) copy-start(bf16[24,400]{1,0:T(8,128)(2,1)S(1)} %get-tuple-element.244) | copy-start | bytes 57604
  391.7 332.2 %copy-start.451 = (bf16[24,400]{1,0:T(8,128)(2,1)}, bf16[24,400]{1,0:T(8,128)(2,1)S(1)}, u32[]{:S(2)}) copy-start(bf16[24,400]{1,0:T(8,128)(2,1)S(1)} %get-tuple-element.198) | copy-start | bytes 57604
  402.1 314.9 %copy-start.395 = (bf16[24,400]{1,0:T(8,128)(2,1)}, bf16[24,400]{1,0:T(8,128)(2,1)S(1)}, u32[]{:S(2)}) copy-start(bf16[24,400]{1,0:T(8,128)(2,1)S(1)} %get-tuple-element.246) | copy-start | bytes 57604
  408.3 315.9 %copy-start.453 = (bf16[24,400]{1,0:T(8,128)(2,1)}, bf16[24,400]{1,0:T(8,128)(2,1)S(1)}, u32[]{:S(2)}) copy-start(bf16[24,400]{1,0:T(8,128)(2,1)S(1)} %get-tuple-element.200) | copy-start | bytes 57604
  419.3 298.0 %copy-start.397 = (bf16[24,400]{1,0:T(8,128)(2,1)}, bf16[24,400]{1,0:T(8,128)(2,1)S(1)}, u32[]{:S(2)}) copy-start(bf16[24,400]{1,0:T(8,128)(2,1)S(1)} %get-tuple-element.248) | copy-start | bytes 57604
  425.5 299.0 %copy-start.455 = (bf16[24,400]{1,0:T(8,128)(2,1)}, bf16[24,400]{1,0:T(8,128)(2,1)S(1)}, u32[]{:S(2)}) copy-start(bf16[24,400]{1,0:T(8,128)(2,1)S(1)} %get-tuple-element.202) | copy-start | bytes 57604
  436.7 280.9 %copy-start.399 = (bf16[24,400]{1,0:T(8,128)(2,1)}, bf16[24,400]{1,0:T(8,128)(2,1)S(1)}, u32[]{:S(2)}) copy-start(bf16[24,400]{1,0:T(8,128)(2,1)S(1)} %get-tuple-element.250) | copy-start | bytes 57604
  442.8 282.0 %copy-start.457 = (bf16[24,400]{1,0:T(8,128)(2,1)}, bf16[24,400]{1,0:T(8,128)(2,1)S(1)}, u32[]{:S(2)}) copy-start(bf16[24,400]{1,0:T(8,128)(2,1)S(1)} %get-tuple-element.204) | copy-start | bytes 57604
  454.4 263.5 %copy-start.401 = (bf16[24,400]{1,0:T(8,128)(2,1)}, bf16[24,400]{1,0:T(8,128)(2,1)S(1)}, u32[]{:S(2)}) copy-start(bf16[24,400]{1,0:T(8,128)(2,1)S(1)} %get-tuple-element.252) | copy-start | bytes 57604
  460.4 264.7 %copy-start.459 = (bf16[24,400]{1,0:T(8,128)(2,1)}, bf16[24,400]{1,0:T(8,128)(2,1)S(1)}, u32[]{:S(2)}) copy-start(bf16[24,400]{1,0:T(8,128)(2,1)S(1)} %get-tuple-element.206) | copy-start | bytes 57604
  472.6 245.6 %copy-start.403 = (bf16[24,400]{1,0:T(8,128)(2,1)}, bf16[24,400]{1,0:T(8,128)(2,1)S(1)}, u32[]{:S(2)}) copy-start(bf16[24,400]{1,0:T(8,128)(2,1)S(1)} %get-tuple-element.254) | copy-start | bytes 57604
  491.5 227.1 %copy-start.405 = (bf16[24,400]{1,0:T(8,128)(2,1)}, bf16[24,400]{1,0:T(8,128)(2,1)S(1)}, u32[]{:S(2)}) copy-start(bf16[24,400]{1,0:T(8,128)(2,1)S(1)} %get-tuple-element.256) | copy-start | bytes 57604
  (1005 other events, 4904.0 us)
Sparse Core Ops, SparseCore 0:
  738.8 131.4 all-reduce.5
where the time goes:
time: 894 us; the launch traced here: 881 us
  matrix products  538 us (60%)
  other arithmetic  133 us (15%)
  waiting for transfers between devices  66 us (7%)
  local copies, waits for them, and re-layouts  55 us (6%)
  blocking collectives  54.4 us (6%)
  between operations  34.3 us (4%)
    psum x1, waiting for transfers between devices, per_device(): lax.psum((sums[0], sums[1], sums[2], sums[3], sums[4]), ('tm', 'batch'))  65.9 us
    dot_general x46, matrix products, run_block(): jnp.einsum('bih,bh->bi', earlier, first_act, precision=EXACT) * decays  63.8 us
    dot_general x46, matrix products, back_block(): jnp.einsum('bih,bh->bi', earlier, d_mix, precision=EXACT) * decays  63.8 us
    dot_general x44, matrix products, back_block(): jnp.einsum('bih,bh->bi', later_first, p_now, precision=EXACT) * ahead  63.8 us
    dot_general x44, matrix products, back_block(): jnp.einsum('bih,bh->bi', later_mix, p_now, precision=EXACT) * ahead  60.5 us
    dot_general x46, matrix products, run_block(): jnp.einsum('bi,bih->bh', coef_row, earlier, precision=EXACT)  43 us
    dot_general x46, matrix products, back_block(): jnp.einsum('bi,bih->bh', coef_row, earlier, precision=EXACT)  42.6 us
    dot_general x44, matrix products, back_block(): jnp.einsum('bi,bih->bh', mix_coef, later_first, precision=EXACT)  41.7 us

commit v1 on v0

v1 whole, which is shorter than its diff:
```python
import functools, math
import jax, jax.numpy as jnp
from jax import lax
from jax.experimental import pallas as pl
from jax.experimental.pallas import tpu as pltpu
from jax.sharding import PartitionSpec as P
F32, BF16 = jnp.float32, jnp.bfloat16
DECAY, RATE, EPS = 0.95, 0.5, 1e-5
B, T, TV, H, E = 48, 24, 21, 400, 100
HP = 512
LT = H // 128 * 128
OFF = H - LT
SUB = 8

def kappa(i):
    return math.sqrt(RATE) * DECAY ** (-i / 2)

def body(cfg, x_ref, len_ref, cot_ref, wc_ref, gain_ref, shift_ref,
         hid_out, gx_out, g_out,
         xs, xr, cotf, hidf, hx, first_s, slope_s, s_s, xh_s, rstd_s, pt_s, pc_s, f_s, dpre_s, dmix_s, mt_s, gain_acc, shift_acc, gain_p, shift_p):
    chains = cfg["chains"]
    NG = B // SUB
    lane = lax.broadcasted_iota(jnp.int32, (SUB, 128), 1)
    hmask = (lax.broadcasted_iota(jnp.int32, (SUB, HP), 1) < H)
    xs[:, :E] = x_ref[...].astype(F32)
    def prep(i, _):
        r = pl.ds(pl.multiple_of(i * 48, 48), 48)
        v = pltpu.roll(xs[r, :], OFF, 1)
        l = lax.broadcasted_iota(jnp.int32, (48, 128), 1)
        xr[r, :] = jnp.where(l < OFF + E, v, jnp.where(l < OFF + E + 3, 1.0, 0.0))
        for k in range(3):
            cotf[k, r, :] = cot_ref[r, k * 128:(k + 1) * 128].astype(F32)
        cotf[3, r, :] = jnp.zeros((48, 128), F32)
        cotf[3, r, :OFF] = cot_ref[r, LT:].astype(F32)
        return 0
    lax.fori_loop(0, B * T // 48, prep, 0)
    zero8 = jnp.zeros((SUB, HP), F32)
    for padded, ref in ((gain_p, gain_ref), (shift_p, shift_ref)):
        padded[...] = jnp.zeros((SUB, HP), F32)
        padded[:, :H] = jnp.broadcast_to(ref[...], (SUB, H))
    gain, shift = gain_p[...], shift_p[...]
    lens = [jnp.broadcast_to(len_ref[g * SUB:(g + 1) * SUB, :], (SUB, 128)) for g in range(NG)]
    def valid(g, t):
        m = lens[g] > t
        return jnp.concatenate([m] * 4, 1)
    def bl(c):
        return jnp.broadcast_to(c, (SUB, HP))
    def rows(g): return slice(g * SUB, (g + 1) * SUB)
    h = [zero8] * NG
    for t in range(TV):
        dec = DECAY ** t
        for r0, nr in chains:
            gs = range(r0 // SUB, (r0 + nr) // SUB)
            xt = xr[pl.ds(r0 * T + t, nr, stride=T), :]
            hv = jnp.concatenate([h[g] for g in gs], 0)
            l = lax.broadcasted_iota(jnp.int32, (nr, 128), 1)
            hv = jnp.concatenate([hv[:, :LT], jnp.where(l < OFF, hv[:, LT:], xt)], 1).astype(BF16)
            hx[t * B + r0: t * B + r0 + nr, :] = hv
            if t == 0:
                u = jnp.dot(hv[:, LT:], wc_ref[LT:, :], preferred_element_type=F32)
            else:
                u = jnp.dot(hv, wc_ref[...], preferred_element_type=F32)
            cs = {}
            us = {}
            for k, g in enumerate(gs):
                ug = u[k * SUB:(k + 1) * SUB, :]
                us[g] = ug
                sg = jax.nn.sigmoid(ug)
                first = ug * sg
                slope_s[t, rows(g), :] = (sg + first * (1.0 - sg)) * dec
                first = first * dec
                first_s[t, rows(g), :] = first
                cs[g] = []
                for i in range(1, t + 1):
                    c = jnp.sum(pt_s[i, rows(g), :] * first, -1, keepdims=True)
                    f_s[t * (t - 1) // 2 + i - 1, rows(g), :] = jnp.broadcast_to(c, (SUB, 128))
                    cs[g].append(c)
            for k, g in enumerate(gs):
                ug = us[g]
                mu = jnp.sum(ug, -1, keepdims=True) * (1.0 / H)
                mc = jnp.where(hmask, ug - bl(mu), 0.0)
                for i in range(1, t + 1):
                    mc = mc + bl(cs[g][i - 1]) * pc_s[i, rows(g), :]
                var = jnp.sum(mc * mc, -1, keepdims=True) * (1.0 / H)
                rstd = lax.rsqrt(var + EPS)
                xh = mc * bl(rstd)
                z = xh * gain + shift
                sz = jax.nn.sigmoid(z)
                out = z * sz
                xh_s[t, rows(g), :] = xh
                rstd_s[t, rows(g), :] = jnp.broadcast_to(rstd, (SUB, 128))
                s_s[t, rows(g), :] = sz + out * (1.0 - sz)
                h[g] = jnp.where(valid(g, t), out, h[g])
                for tt in ([t] if t < TV - 1 else range(t, T)):
                    for k4 in range(4):
                        hidf[k4, pl.ds(g * SUB * T + tt, SUB, stride=T), :] = h[g][:, k4 * 128:(k4 + 1) * 128]
                if t < TV - 1:
                    pt = h[g] * kappa(t + 1)
                    pt_s[t + 1, rows(g), :] = pt
                    mp = jnp.sum(pt, -1, keepdims=True) * (1.0 / H)
                    pc_s[t + 1, rows(g), :] = jnp.where(hmask, pt - bl(mp), 0.0)
    def cot(g, t):
        return jnp.concatenate([cotf[k, pl.ds(g * SUB * T + t, SUB, stride=T), :] for k in range(4)], 1)
    grad = []
    for g in range(NG):
        a = cot(g, T - 1)
        for t in range(T - 2, TV - 1, -1):
            a = a + cot(g, t)
        grad.append(a)
        gain_acc[rows(g), :] = jnp.zeros((SUB, HP), F32)
        shift_acc[rows(g), :] = jnp.zeros((SUB, HP), F32)
    for t in range(TV - 1, -1, -1):
        for r0, nr in chains:
            gs = range(r0 // SUB, (r0 + nr) // SUB)
            passed, dmixs, ms, dpres = {}, {}, {}, {}
            for g in gs:
                tot = grad[g] + cot(g, t)
                D = jnp.where(valid(g, t), tot, 0.0)
                passed[g] = tot
                xh = xh_s[t, rows(g), :]
                dz = D * s_s[t, rows(g), :]
                gain_acc[rows(g), :] += dz * xh
                shift_acc[rows(g), :] += dz
                dxh = dz * gain
                m1 = jnp.sum(dxh, -1, keepdims=True) * (1.0 / H)
                m2 = jnp.sum(dxh * xh, -1, keepdims=True) * (1.0 / H)
                rstd = rstd_s[t, rows(g), :]
                dmix = jnp.concatenate([rstd] * 4, 1) * (dxh - bl(m1) - xh * bl(m2))
                dmixs[g] = dmix
                dmix_s[t, rows(g), :] = dmix
            for g in gs:
                ms[g] = []
                for i in range(1, t + 1):
                    c = jnp.sum(pt_s[i, rows(g), :] * dmixs[g], -1, keepdims=True)
                    ms[g].append(c)
                    mt_s[t * (t - 1) // 2 + i - 1, rows(g), :] = jnp.broadcast_to(c, (SUB, 128))
            for g in gs:
                if t > 0:
                    df = bl(ms[g][0]) * pt_s[1, rows(g), :]
                    for i in range(2, t + 1):
                        df = df + bl(ms[g][i - 1]) * pt_s[i, rows(g), :]
                    dpres[g] = dmixs[g] + df * slope_s[t, rows(g), :]
                else:
                    dpres[g] = dmixs[g]
            dp = jnp.concatenate([dpres[g] for g in gs], 0).astype(BF16)
            dpre_s[t * B + r0: t * B + r0 + nr, :] = dp
            fr = lax.dot_general(dp, wc_ref[...] if t > 0 else wc_ref[LT:, :], (((1,), (1,)), ((), ())), preferred_element_type=F32)
            gxt = fr[:, -128:]
            xs[pl.ds(r0 * T + t, nr, stride=T), :] = pltpu.roll(gxt, 128 - OFF, 1)
            if t > 0:
                for k, g in enumerate(gs):
                    S = None
                    for kk in range(TV - 1, t - 1, -1):
                        q = kk * (kk - 1) // 2 + t - 1
                        fc = f_s[q, rows(g), :]
                        mc_ = mt_s[q, rows(g), :] if kk > t else ms[g][t - 1]
                        fc = jnp.concatenate([fc] * 4, 1)
                        mc_ = jnp.concatenate([mc_] * 4, 1) if kk > t else bl(mc_)
                        term = fc * (dmix_s[kk, rows(g), :] if kk > t else dmixs[g]) + mc_ * first_s[kk, rows(g), :]
                        S = term if S is None else S + term
                    new = fr[k * SUB:(k + 1) * SUB, :] + S * kappa(t)
                    grad[g] = jnp.where(valid(g, t), new, passed[g])
        if t % 5 == 1:
            a = hx[t * B:(t + 5) * B, :]
            d = dpre_s[t * B:(t + 5) * B, :]
            prod = lax.dot_general(a, d, (((0,), (0,)), ((), ())), preferred_element_type=F32)
            if t + 5 == TV:
                g_out[...] = prod
            else:
                g_out[...] += prod
        if t == 0:
            prod = lax.dot_general(hx[:B, LT:], dpre_s[:B, :], (((0,), (0,)), ((), ())), preferred_element_type=F32)
            g_out[LT:, :] += prod
    g_out[HP - 8:, :] = jnp.concatenate([
        g_out[HP - 8:HP-7,:]*0, g_out[HP - 7:HP-6,:]*0,
        jnp.sum(gain_acc[...], 0, keepdims=True), jnp.sum(shift_acc[...], 0, keepdims=True), jnp.zeros((4, HP), F32)], 0)
    for t in range(TV, T):
        xs[pl.ds(t, B, stride=T), :] = jnp.zeros((B, 128), F32)
    def fin(i, _):
        r = pl.ds(pl.multiple_of(i * 48, 48), 48)
        for k in range(3):
            hid_out[r, k * 128:(k + 1) * 128] = hidf[k, r, :].astype(BF16)
        hid_out[r, LT:] = hidf[3, r, :OFF].astype(BF16)
        gx_out[r, :] = xs[r, :E]
        return 0
    lax.fori_loop(0, B * T // 48, fin, 0)


MESH = pl.DeviceIdType.MESH


def gather_body(w_ref, c_ref, bias_ref, wc_out, blk, brow, ssem, xsem, fsem, rsem, xrsem, frsem):
    me, b = lax.axis_index("tm"), lax.axis_index("batch")
    sib, xp = lax.bitwise_xor(me, 1), lax.bitwise_xor(me, 2)
    diag = lax.bitwise_xor(me, 3)
    barrier = pltpu.get_barrier_semaphore()
    for peer in (sib, xp):
        pl.semaphore_signal(barrier, inc=1, device_id=(peer, b), device_id_type=MESH)
    blk[me] = jnp.zeros((HP, 128), BF16)
    blk[me, :H, :E] = w_ref[...]
    blk[me, H:H + E, :E] = c_ref[...]
    brow[...] = jnp.zeros((SUB, HP), F32)
    brow[:1, :H] = bias_ref[...]
    pl.semaphore_wait(barrier, 2)
    def half(ref_slot, i):
        return blk.at[ref_slot, pl.ds(i * 256, 256)]
    xcopies = []
    for i in range(2):
        cp = pltpu.make_async_remote_copy(src_ref=half(me, i), dst_ref=half(me, i), send_sem=xsem.at[i], recv_sem=xrsem.at[i],
            device_id=(xp, b), device_id_type=MESH)
        cp.start()
        xcopies.append(cp)
    own = pltpu.make_async_remote_copy(src_ref=blk.at[me], dst_ref=blk.at[me], send_sem=ssem, recv_sem=rsem,
        device_id=(sib, b), device_id_type=MESH)
    own.start()
    fcopies = []
    for i in range(2):
        xcopies[i].wait_recv()
        cp = pltpu.make_async_remote_copy(src_ref=half(xp, i), dst_ref=half(xp, i), send_sem=fsem.at[i], recv_sem=frsem.at[i],
            device_id=(sib, b), device_id_type=MESH)
        cp.start()
        fcopies.append(cp)
    own.wait_recv()
    for i in range(2):
        fcopies[i].wait_recv()
    own.wait_send()
    for i in range(2):
        xcopies[i].wait_send()
        fcopies[i].wait_send()
    row = lax.broadcasted_iota(jnp.int32, (16, HP), 0)
    bias = jnp.broadcast_to(brow[:1, :], (16, HP))
    hi = bias.astype(BF16).astype(F32)
    mid = (bias - hi).astype(BF16).astype(F32)
    lo = bias - hi - mid
    for r in range(0, HP, 64):
        l = lax.broadcasted_iota(jnp.int32, (64, 128), 1)
        b0, b1, b2, b3 = [blk[k, r:r + 64, :].astype(F32) for k in range(4)]
        b1, b2, b3 = pltpu.roll(b1, 100, 1), pltpu.roll(b2, 72, 1), pltpu.roll(b3, 44, 1)
        wc_out[r:r + 64, 0:128] = jnp.where(l < 100, b0, b1).astype(BF16)
        wc_out[r:r + 64, 128:256] = jnp.where(l < 72, b1, b2).astype(BF16)
        wc_out[r:r + 64, 256:384] = jnp.where(l < 44, b2, b3).astype(BF16)
        wc_out[r:r + 64, 384:512] = jnp.where(l < 16, b3, 0.0).astype(BF16)
    last = wc_out[HP - 16:, :].astype(F32)
    last = jnp.where(row == 4, hi, jnp.where(row == 5, mid, jnp.where(row == 6, lo, jnp.where(row < 4, last, 0.0))))
    wc_out[HP - 16:, :] = last.astype(BF16)


def gather_call(w, c, bias):
    D = pltpu.SemaphoreType.DMA
    return pl.pallas_call(
        gather_body,
        out_shape=jax.ShapeDtypeStruct((HP, HP), BF16),
        scratch_shapes=[pltpu.VMEM((4, HP, 128), BF16), pltpu.VMEM((SUB, HP), F32), D, D((2,)), D((2,)), D, D((2,)), D((2,))],
        compiler_params=pltpu.CompilerParams(collective_id=0, has_side_effects=True, vmem_limit_bytes=60 * 2**20),
    )(w, c, bias.reshape(1, H))


def reduce_body(nb, g_ref, gw_out, gc_out, v_out, blk, pk, sib_in, rs_out, rs_in, ag, ssem, srsem, rsem_s, rsem_r, asem_s, asem_r):
    me, b = lax.axis_index("tm"), lax.axis_index("batch")
    core, sib = lax.rem(me, 2), lax.bitwise_xor(me, 1)
    xi = me // 2
    piece = HP // nb
    barrier = pltpu.get_barrier_semaphore()
    pl.semaphore_signal(barrier, inc=1, device_id=(sib, b), device_id_type=MESH)
    others = [(dx, db) for db in range(nb) for dx in range(2) if dx or db]
    base = b // nb * nb
    rank = b - base
    def peer(dx, db):
        return lax.rem(xi + dx, 2), base + lax.rem(rank + db, nb)
    for dx, db in others:
        px, pb = peer(dx, db)
        pl.semaphore_signal(barrier, inc=1, device_id=(2 * px + core, pb), device_id_type=MESH)
    l = lax.broadcasted_iota(jnp.int32, (64, 128), 1)
    for r in range(0, HP, 64):
        t0, t1, t2, t3 = [g_ref[r:r + 64, k * 128:(k + 1) * 128] for k in range(4)]
        out = [t0,
            jnp.where(l < 28, pltpu.roll(t0, 28, 1), pltpu.roll(t1, 28, 1)),
            jnp.where(l < 56, pltpu.roll(t1, 56, 1), pltpu.roll(t2, 56, 1)),
            jnp.where(l < 84, pltpu.roll(t2, 84, 1), pltpu.roll(t3, 84, 1))]
        for k in range(4):
            blk[k, r:r + 64, :] = out[k]
            pk[k, r:r + 64, :] = out[k].astype(BF16)
    pl.semaphore_wait(barrier, len(others) + 1)
    scopies = []
    for j in range(2):
        k = 2 * j + (1 - core)
        cp = pltpu.make_async_remote_copy(src_ref=pk.at[k], dst_ref=sib_in.at[j], send_sem=ssem.at[j], recv_sem=srsem.at[j],
            device_id=(sib, b), device_id_type=MESH)
        cp.start()
        scopies.append(cp)
    for j in range(2):
        scopies[j].wait_recv()
        for r in range(0, HP, 64):
            rs_out[j, r:r + 64, :] = (blk[2 * j + core, r:r + 64, :] + sib_in[j, r:r + 64, :].astype(F32)).astype(BF16)
    rcopies = []
    for n, (dx, db) in enumerate(others):
        px, pb = peer(dx, db)
        slot = dx * nb + db
        cp = pltpu.make_async_remote_copy(src_ref=rs_out.at[px, pl.ds(pl.multiple_of((pb - base) * piece, piece), piece)], dst_ref=rs_in.at[slot],
            send_sem=rsem_s.at[slot], recv_sem=rsem_r.at[slot], device_id=(2 * px + core, pb), device_id_type=MESH)
        cp.start()
        rcopies.append(cp)
    total = rs_out[xi, pl.ds(pl.multiple_of(rank * piece, piece), piece), :].astype(F32)
    for n, (dx, db) in enumerate(others):
        rcopies[n].wait_recv()
        total = total + rs_in[dx * nb + db].astype(F32)
    ag[rank] = total.astype(BF16)
    acopies = []
    for db in range(1, nb):
        pb = base + lax.rem(rank + db, nb)
        cp = pltpu.make_async_remote_copy(src_ref=ag.at[rank], dst_ref=ag.at[rank], send_sem=asem_s.at[db], recv_sem=asem_r.at[db],
            device_id=(me, pb), device_id_type=MESH)
        cp.start()
        acopies.append(cp)
    for cp in acopies:
        cp.wait_recv()
    for j in range(nb):
        v = ag[j].astype(F32)
        for r in range(0, piece, 8):
            row = j * piece + r
            blk[0, row:row + 8, :] = v[r:r + 8, :]
    gw_out[...] = blk[0, :H, :E]
    gc_out[...] = blk[0, H:H + E, :E]
    v_out[...] = blk[0, HP - 16:, :E]
    for cp in scopies + rcopies + acopies:
        cp.wait_send()


def reduce_call(g, nb):
    D = pltpu.SemaphoreType.DMA
    V = pltpu.VMEM
    piece = HP // nb
    return pl.pallas_call(
        functools.partial(reduce_body, nb),
        out_shape=(jax.ShapeDtypeStruct((H, E), F32), jax.ShapeDtypeStruct((E, E), F32), jax.ShapeDtypeStruct((16, E), F32)),
        scratch_shapes=[V((4, HP, 128), F32), V((4, HP, 128), BF16), V((2, HP, 128), BF16), V((2, HP, 128), BF16),
            V((2 * nb, piece, 128), BF16), V((nb, piece, 128), BF16),
            D((2,)), D((2,)), D((2 * nb,)), D((2 * nb,)), D((nb,)), D((nb,))],
        compiler_params=pltpu.CompilerParams(collective_id=1, has_side_effects=True, vmem_limit_bytes=60 * 2**20),
    )(g)


def cell_call(x, lengths, cot, wc, gain, shift):
    NP = TV * (TV - 1) // 2
    V = pltpu.VMEM
    return pl.pallas_call(
        functools.partial(body, dict(chains=[(0, 16), (16, 16), (32, 16)])),
        out_shape=(jax.ShapeDtypeStruct((B * T, H), BF16), jax.ShapeDtypeStruct((B * T, E), F32), jax.ShapeDtypeStruct((HP, HP), F32)),
        scratch_shapes=[V((B * T, 128), F32), V((B * T, 128), F32), V((4, B * T, 128), F32), V((4, B * T, 128), F32),
            V((TV * B, HP), BF16), V((TV, B, HP), F32), V((TV, B, HP), F32), V((TV, B, HP), F32), V((TV, B, HP), F32), V((TV, B, 128), F32),
            V((TV, B, HP), F32), V((TV, B, HP), F32), V((NP, B, 128), F32), V((TV * B, HP), BF16), V((TV, B, HP), F32), V((NP, B, 128), F32),
            V((B, HP), F32), V((B, HP), F32), V((SUB, HP), F32), V((SUB, HP), F32)],
        compiler_params=pltpu.CompilerParams(vmem_limit_bytes=60 * 2**20),
    )(x.reshape(B * T, E), lengths.reshape(B, 1), cot.reshape(B * T, H), wc, gain.reshape(1, H), shift.reshape(1, H))


def per_device(inputs, lengths, w_rec, w_in, rec_bias, norm_gain, norm_shift, cotangent, nb):
    wc = gather_call(w_rec, w_in, rec_bias)
    hid, gx, g = cell_call(inputs, lengths, cotangent, wc, norm_gain, norm_shift)
    group = math.gcd(nb, 8)
    parts = reduce_call(g, group)
    if nb > group:
        parts = [lax.all_gather(p, "batch").reshape(nb // group, group, *p.shape)[:, 0].sum(0) for p in parts]
    gw, gc, v = parts
    return hid.reshape(B, T, H), gx.reshape(B, T, E), gw, gc, v[4], v[10], v[11]


def solution(mesh):
    both = ("tm", "batch")
    return jax.shard_map(
        functools.partial(per_device, nb=mesh.shape["batch"]),
        mesh=mesh,
        in_specs=(P(both, None, None), P(both), P(None, "tm"), P(None, "tm"), P(), P(), P(), P(both, None, None)),
        out_specs=(P(both, None, None), P(both, None, None), P(None, "tm"), P(None, "tm"), P("tm"), P("tm"), P("tm")),
        check_vma=False,
    )
```

time: 894 us -> 65.2 us (0.07); the launches traced: 881 us -> 64.9 us
  matrix products: 538 us -> 0 us
  other arithmetic: 133 us -> 0 us
  waiting for transfers between devices: 66 us -> 0 us
  Pallas kernels: 0 us -> 58.5 us
  blocking collectives: 54.4 us -> 0 us
  local copies, waits for them, and re-layouts: 55 us -> 5.67 us
  between operations: 34.3 us -> 0.65 us
    dot_general x645 -> x0, matrix products: 538 us -> none  [the longest x46 63.8 us: run_block(): jnp.einsum('bih,bh->bi', earlier, first_act, precision=EXACT) * decays]
    reduce_sum x184 -> x0, other arithmetic: 68.5 us -> none  [the longest x46 37.7 us: back_block(): bias_sum = bias_sum + jnp.sum(d_pre.astype(jnp.float32), 0)]
    psum x1 -> x0, waiting for transfers between devices: 65.9 us -> none  [per_device(): lax.psum((sums[0], sums[1], sums[2], sums[3], sums[4]), ('tm', 'batch'))]
    pallas_call x0 -> x3, Pallas kernels: none -> 58.5 us  [the longest x1 26.8 us: cell_call(): pl.pallas_call(functools.partial(body, dict(chains=[(0, 16), (16, 16), (3...]
    psum x1 -> x0, blocking collectives: 40.8 us -> none  [per_device(): lax.psum((sums[0], sums[1], sums[2], sums[3], sums[4]), ('tm', 'batch'))]
    unnamed x2276 -> x2, local copies, waits for them, and re-layouts: 41.3 us -> 3.06 us
    unnamed x472 -> x0, other arithmetic: 34.2 us -> none
    all_gather x2 -> x0, blocking collectives: 13.6 us -> none  [the longest x1 7.22 us: per_device(): lax.all_gather(w_rec, 'tm', axis=1, tiled=True)]
where the time goes in v1:
time: 65.2 us; the launch traced here: 64.9 us
  Pallas kernels  58.5 us (90%)
  local copies, waits for them, and re-layouts  5.67 us (9%)
    pallas_call x1, Pallas kernels, cell_call(): pl.pallas_call(functools.partial(body, dict(chains=[(0, 16), (16, 16), (3...  26.8 us
    pallas_call x1, Pallas kernels, reduce_call(): pl.pallas_call(functools.partial(reduce_body, nb), out_shape=(jax.ShapeDt...  21.7 us
    pallas_call x1, Pallas kernels, gather_call(): pl.pallas_call(gather_body, out_shape=jax.ShapeDtypeStruct((HP, HP), BF16...  9.99 us
    unnamed x2, local copies, waits for them, and re-layouts  3.06 us
    reshape x1, local copies, waits for them, and re-layouts, cell_call(): lengths.reshape(B, 1)  1.35 us

profile of v1, /device:TPU:0, one launch (start us, length us, event | category | flops | bytes accessed | tf_op | source)
XLA Modules:
  0.0 64.9 jit_solution(14494788482460614894)
XLA Ops:
  0.6 1.3 %copy.15.len_ref = s32[48,1]{1,0:T(8,128)} copy(s32[48,1]{0,1:T(1,128)} %bitcast.19) | data formatting | bytes 384 | tf_op jit(solution)/shard_map/reshape | solution.py:354
  2.0 10.0 %shard_map.135.wc_ref = bf16[512,512]{1,0:T(8,128)(2,1)} custom-call(bf16[400,100]{1,0:T(8,128)(2,1)} %w_ref.1, bf16[100,100]{1,0:T(8,128)(2,1)} %c_ref.1, f32[1,400]{1,0:T(1,128)} %bitcast.16), custom_call_target="tpu_custom_call" | custom-call | tf_op jit(solution)/shard_map/pallas_call | solution.py:250
  12.0 26.8 %shard_map.136 = (bf16[1152,400]{1,0:T(8,128)(2,1)}, f32[1152,100]{1,0:T(8,128)}, f32[512,512]{1,0:T(8,128)}) custom-call(bf16[1152,100]{1,0:T(8,128)(2,1)} %bitcast.15, s32[48,1]{1,0:T(8,128)} %copy.15.len_ref, bf16[1152,400]{1,0:T(8,128)(2,1)} %bitcast.14, bf16[512,512]{1,0:T(8,128)(2,1)} %shard_map.135.wc_ref, f32[1,400]{1,0:T(1,128)} %bitcast.17, ...), custom_call_target="tpu_custom_call" | custom-call | tf_op jit(solution)/shard_map/pallas_call | solution.py:346
  38.8 21.7 %shard_map.137 = (f32[400,100]{1,0:T(8,128)}, f32[100,100]{1,0:T(8,128)}, f32[16,100]{1,0:T(8,128)}) custom-call(f32[512,512]{1,0:T(8,128)} %get-tuple-element.15.g_ref), custom_call_target="tpu_custom_call" | custom-call | tf_op jit(solution)/shard_map/pallas_call | solution.py:333
  60.5 1.3 %slice_bitcast_fusion = (f32[100]{0:T(128)}, f32[100]{0:T(128)}, f32[100]{0:T(128)}) fusion(f32[16,100]{1,0:T(8,128)} %get-tuple-element.18), kind=kLoop, calls=%fused_computation | loop fusion | bytes 2400 | tf_op jit(solution)/shard_map/squeeze | solution.py:365
  61.8 1.6 %copy.18 = f32[400,100]{1,0:T(8,128)} copy(f32[400,100]{1,0:T(8,128)} %get-tuple-element.31) | data formatting | bytes 320000
  63.4 1.4 %copy.19 = f32[100,100]{1,0:T(8,128)} copy(f32[100,100]{1,0:T(8,128)} %get-tuple-element.32) | data formatting | bytes 80000

commit v2 on v0

v2 whole, which is shorter than its diff:
```python
import functools, math
import jax, jax.numpy as jnp
from jax import lax
from jax.experimental import pallas as pl
from jax.experimental.pallas import tpu as pltpu
from jax.sharding import PartitionSpec as P
F32, BF16 = jnp.float32, jnp.bfloat16
DECAY, RATE, EPS = 0.95, 0.5, 1e-5
B, T, TV, H, E = 48, 24, 21, 400, 100
HP = 512
NT = 4
LT = H // 128 * 128
OFF = H - LT
SUB = 8
ROWS = 16
NC = B // ROWS
NP = TV * (TV - 1) // 2
ONES = 3
LEAST = 5

def kappa(i):
    return math.sqrt(RATE) * DECAY ** (-i / 2)

def tri(t, i):
    return t * (t - 1) // 2 + i - 1

PLANS = ((21, 21, 19, 17, 14, 11), (TV,) * (B // SUB))


def cell_body(info, xs_in, lens_ref, cotf_in, wc_ref, gain_p, shift_p, hid_out, gx_out, hx, dpre_s, sums_out, xs, cotf, gxs, hidf, h_s, *rest):
    accs = [pltpu.ACC(m)((ROWS, 256), F32) for _ in range(NC) for m in range(2)]
    def place(row, n):
        return pl.ds(pl.multiple_of(info[row, n] * T, SUB), T)
    for r in range(B):
        xs[r * T:(r + 1) * T, :] = xs_in[place(1, r), :]
    h_s[...] = jnp.zeros((B, HP), F32)
    sums_out[...] = jnp.zeros((2 * SUB, HP), F32)
    def scoped(*a):
        def run(ends):
            cell_inner(ends, place, xs, lens_ref, cotf_in, wc_ref, gain_p, shift_p, hid_out, hx, dpre_s, sums_out,
                cotf, gxs, hidf, h_s, *rest, [a[2 * i:2 * i + 2] for i in range(NC)])
        lax.cond(info[2, 0] > 0, lambda: run(PLANS[0]), lambda: run(PLANS[1]))
    pl.run_scoped(scoped, *accs)
    for b in range(B):
        gx_out[b * T:(b + 1) * T, :] = gxs[place(0, b), :E]


def cell_inner(ends, place, xs, lens_ref, cotf_in, wc_ref, gain_p, shift_p, hid_out, hx, dpre_s, sums_out,
        cotf, gxs, hidf, h_s, grad_s, first_s, slope_s, s_s, xh_s, rstd_s, pt_s, pc_s, f_s, mt_s, dmix_s, accs):
    lane = lax.broadcasted_iota(jnp.int32, (SUB, 128), 1)
    lane16 = lax.broadcasted_iota(jnp.int32, (ROWS, 128), 1)
    tail = lane < OFF
    zero = jnp.zeros((SUB, 128), F32)
    zb = jnp.zeros((ROWS, HP), BF16)
    def chains(t): return [c for c in range(NC) if ends[2 * c] > t]
    def groups(c, t): return [g for g in (2 * c, 2 * c + 1) if ends[g] > t]
    def rows(g): return slice(g * SUB, (g + 1) * SUB)
    def crow(c): return slice(c * ROWS, (c + 1) * ROWS)
    def cut(k): return slice(k * 128, (k + 1) * 128)
    def ld(ref, t, g): return [ref[t, rows(g), cut(k)] for k in range(NT)]
    def st(ref, t, g, v):
        for k in range(NT):
            ref[t, rows(g), cut(k)] = v[k]
    def lsum(v):
        return jnp.broadcast_to(jnp.sum((v[0] + v[1]) + (v[2] + v[3]), -1, keepdims=True), (SUB, 128))
    def only_h(v): return [v[0], v[1], v[2], jnp.where(tail, v[3], 0.0)]
    def push(k, transpose):
        for m in range(2):
            if transpose:
                w = wc_ref[m * 256:(m + 1) * 256, k * 256:(k + 1) * 256]
            else:
                w = wc_ref[k * 256:(k + 1) * 256, m * 256:(m + 1) * 256]
            pltpu.matmul_push_rhs(w, k, m, transpose=transpose)
    def mm(c, v, transpose, last, after):
        lhs = [jnp.concatenate(v[:2], 1), jnp.concatenate(v[2:], 1)]
        o = (0, 1) if c % 2 == 0 else (1, 0)
        for n, k in enumerate(o):
            for m in range(2):
                pltpu.matmul_acc_lhs(accs[c][m], lhs[k], load_staged_rhs=k if n or c == 0 else None)
            if n == 0 and c > 0:
                push(o[1], transpose)
        if last and after is not None:
            push(0, after), push(1, after)
    def pop(c):
        u = [pltpu.matmul_pop(accs[c][m]) for m in range(2)]
        return [u[0][:, :128], u[0][:, 128:], u[1][:, :128], u[1][:, 128:]]
    push(0, False), push(1, False)
    def sort_cot(r):
        for k in range(NT):
            cotf[k, r * T:(r + 1) * T, :] = cotf_in[k, place(1, r), :]
    def fin(i):
        r = slice(i * 2 * T, (i + 1) * 2 * T)
        for k in range(NT):
            v = jnp.concatenate([hidf[k, place(0, 2 * i + j), :] for j in range(2)], 0).astype(BF16)
            hid_out[r, k * 128:min((k + 1) * 128, H)] = v[:, :min(128, H - k * 128)]
    def live(g, t):
        return lens_ref[rows(g), :] > t
    def seqs(c, t): return pl.ds(c * ROWS * T + t, ROWS, stride=T)
    def gseqs(g, t): return pl.ds(g * SUB * T + t, SUB, stride=T)
    def step_rows(c, t): return slice(t * B + c * ROWS, t * B + (c + 1) * ROWS)

    def fwd_step(t):
        dec = DECAY ** t
        on = chains(t)
        for c in range(NC):
            if c not in on:
                hx[step_rows(c, t), :] = zb
                continue
            hv = [h_s[crow(c), cut(k)] for k in range(NT)]
            hv[3] = jnp.where(lane16 < OFF, hv[3], xs[seqs(c, t), :])
            hb = [v.astype(BF16) for v in hv]
            for k in range(NT):
                hx[step_rows(c, t), cut(k)] = hb[k]
            mm(c, hb, False, c == on[-1], t == TV - 1)
        if t > 0:
            for c in on:
                for g in groups(c, t):
                    pt = [h_s[rows(g), cut(k)] * kappa(t) for k in range(NT)]
                    st(pt_s, t, g, pt)
                    mp = lsum(pt) * (1.0 / H)
                    st(pc_s, t, g, only_h([v - mp for v in pt]))
        for c in on:
            u16 = pop(c)
            cs, us = {}, {}
            for g in groups(c, t):
                j = g - 2 * c
                u = [v[j * SUB:(j + 1) * SUB, :] for v in u16]
                mu = lsum(u) * (1.0 / H)
                us[g] = only_h([v - mu for v in u])
                sg = [jax.nn.sigmoid(v) for v in u]
                sgd = [v * dec for v in sg]
                first = [a * b for a, b in zip(u, sgd)]
                st(first_s, t, g, first)
                st(slope_s, t, g, [a + f - f * s for a, f, s in zip(sgd, first, sg)])
                cs[g] = []
                for i in range(1, t + 1):
                    cc = lsum([a * b for a, b in zip(ld(pt_s, i, g), first)])
                    f_s[tri(t, i), rows(g), :] = cc
                    cs[g].append(cc)
            for g in groups(c, t):
                mc = us[g]
                for i in range(1, t + 1):
                    mc = [m + cs[g][i - 1] * p for m, p in zip(mc, ld(pc_s, i, g))]
                var = lsum([m * m for m in mc]) * (1.0 / H)
                rstd = lax.rsqrt(var + EPS)
                xh = [m * rstd for m in mc]
                z = [x * gain_p[:, cut(k)] + shift_p[:, cut(k)] for k, x in enumerate(xh)]
                sz = [jax.nn.sigmoid(v) for v in z]
                out = [a * b for a, b in zip(z, sz)]
                new = out
                if t >= LEAST:
                    ok = live(g, t)
                    new = [jnp.where(ok, a, h_s[rows(g), cut(k)]) for k, a in enumerate(out)]
                for k in range(NT):
                    h_s[rows(g), cut(k)] = new[k]
                    for tt in [t] if t < ends[g] - 1 else range(t, T):
                        hidf[k, gseqs(g, tt), :] = new[k]
                st(xh_s, t, g, xh)
                rstd_s[t, rows(g), :] = rstd
                st(s_s, t, g, [a + o - o * a for a, o in zip(sz, out)])

    def bwd_step(t):
        on = chains(t)
        sums = [None, None]
        dmixs, tots, ms = {}, {}, {}
        for c in range(NC):
            if c not in on:
                dpre_s[step_rows(c, t), :] = zb
                gxs[seqs(c, t), :] = jnp.zeros((ROWS, 128), F32)
                continue
            dps = [[zero] * NT, [zero] * NT]
            for g in groups(c, t):
                if t == ends[g] - 1:
                    tot = [cotf[k, gseqs(g, T - 1), :] for k in range(NT)]
                    for tt in range(T - 2, t - 1, -1):
                        tot = [a + cotf[k, gseqs(g, tt), :] for k, a in enumerate(tot)]
                else:
                    tot = [grad_s[rows(g), cut(k)] + cotf[k, gseqs(g, t), :] for k in range(NT)]
                tots[g] = tot
                xh = ld(xh_s, t, g)
                d = tot if t < LEAST else [jnp.where(live(g, t), a, 0.0) for a in tot]
                dz = [a * s for a, s in zip(d, ld(s_s, t, g))]
                gs = [a * b for a, b in zip(dz, xh)]
                sums = [gs, dz] if sums[0] is None else [[a + b for a, b in zip(p, q)] for p, q in zip(sums, (gs, dz))]
                dxh = [a * gain_p[:, cut(k)] for k, a in enumerate(dz)]
                m1 = lsum(dxh) * (1.0 / H)
                m2 = lsum([a * b for a, b in zip(dxh, xh)]) * (1.0 / H)
                rstd = rstd_s[t, rows(g), :]
                dmixs[g] = only_h([rstd * (a - m1 - b * m2) for a, b in zip(dxh, xh)])
                st(dmix_s, t, g, dmixs[g])
            for g in groups(c, t):
                ms[g] = []
                for i in range(1, t + 1):
                    cc = lsum([a * b for a, b in zip(ld(pt_s, i, g), dmixs[g])])
                    mt_s[tri(t, i), rows(g), :] = cc
                    ms[g].append(cc)
            for g in groups(c, t):
                df = None
                for i in range(1, t + 1):
                    term = [ms[g][i - 1] * p for p in ld(pt_s, i, g)]
                    df = term if df is None else [a + b for a, b in zip(df, term)]
                dps[g - 2 * c] = dmixs[g] if df is None else [a + b * s for a, b, s in zip(dmixs[g], df, ld(slope_s, t, g))]
            db = [jnp.concatenate([dps[0][k], dps[1][k]], 0).astype(BF16) for k in range(NT)]
            for k in range(NT):
                dpre_s[step_rows(c, t), cut(k)] = db[k]
            mm(c, db, True, c == on[-1], True if t > 0 else None)
        for c in on:
            Ss = {}
            if t > 0:
                for g in groups(c, t):
                    S = None
                    for kk in range(ends[g] - 1, t - 1, -1):
                        q = tri(kk, t)
                        dm = ld(dmix_s, kk, g) if kk > t else dmixs[g]
                        f, m = f_s[q, rows(g), :], mt_s[q, rows(g), :]
                        term = [f * a + m * b for a, b in zip(dm, ld(first_s, kk, g))]
                        S = term if S is None else [a + b for a, b in zip(S, term)]
                    Ss[g] = [a * kappa(t) for a in S]
            fr = pop(c)
            gxs[seqs(c, t), :] = pltpu.roll(fr[3], 128 - OFF, 1)
            if t > 0:
                for g in groups(c, t):
                    j = g - 2 * c
                    for k in range(NT):
                        v = fr[k][j * SUB:(j + 1) * SUB, :] + Ss[g][k]
                        grad_s[rows(g), cut(k)] = v if t < LEAST else jnp.where(live(g, t), v, tots[g][k])
        for k in range(NT):
            sums_out[:SUB, cut(k)] += sums[0][k]
            sums_out[SUB:, cut(k)] += sums[1][k]

    todo = list(range(B))
    for t in range(TV):
        fwd_step(t)
        n = -(-len(todo) // (TV - t))
        for r in todo[:n]:
            sort_cot(r)
        todo = todo[n:]
    todo = list(range(B // 2))
    for t in range(TV - 1, -1, -1):
        bwd_step(t)
        n = -(-len(todo) // (t + 1))
        for i in todo[:n]:
            fin(i)
        todo = todo[n:]
    for t in range(TV, T):
        gxs[pl.ds(t, B, stride=T), :] = jnp.zeros((B, 128), F32)


def cell_call(info, xs, lens, cotf, wc, gain_p, shift_p):
    V = pltpu.VMEM
    S = jax.ShapeDtypeStruct
    big = V((TV, B, HP), F32)
    pair = V((NP, B, 128), F32)
    seq, wide = V((B * T, 128), F32), V((NT, B * T, 128), F32)
    vs = pl.BlockSpec(memory_space=pltpu.VMEM)
    return pl.pallas_call(
        cell_body,
        out_shape=(S((B * T, H), BF16), S((B * T, E), F32), S((TV * B, HP), BF16), S((TV * B, HP), BF16), S((2 * SUB, HP), F32)),
        in_specs=[pl.BlockSpec(memory_space=pltpu.SMEM)] + [vs] * 6,
        scratch_shapes=[seq, wide, seq, wide, V((B, HP), F32), V((B, HP), F32),
            big, big, big, big, V((TV, B, 128), F32), big, big, pair, pair, big],
        compiler_params=pltpu.CompilerParams(vmem_limit_bytes=44 * 2**20),
    )(info, xs, lens, cotf, wc, gain_p, shift_p)


MESH = pl.DeviceIdType.MESH
PR = 416
XR = 104
Q = 4
QC = E // Q


def pack(main, extra, lane_of):
    pieces = []
    for q in range(Q):
        m = main(q)
        x = pltpu.roll(extra, E - QC * q, 1) if E != QC * q else extra
        pieces.append(jnp.where(lane_of < E, m, jnp.where(lane_of < E + QC, x, 0.0)))
    return pieces


def unpack_extra(block, lane_of):
    out = None
    for q in range(Q):
        x = pltpu.roll(block(q), 128 - E + QC * q, 1)
        keep = (lane_of >= QC * q) & (lane_of < QC * (q + 1))
        out = jnp.where(keep, x, 0.0 if out is None else out)
    return out


def gather_body(w_ref, c_ref, bias_ref, len_ref, x_ref, cot_ref, gain_ref, shift_ref,
        wc_out, info_out, lens_out, xs_out, cotf_out, gain_out, shift_out,
        w_v, c_v, bias_v, len_v, x_v, cot_v, gain_v, shift_v, blk, stage, cst, brow, xpad, ssem, rsem, lsem):
    me, b = lax.axis_index("tm"), lax.axis_index("batch")
    sib, xp, diag = lax.bitwise_xor(me, 1), lax.bitwise_xor(me, 2), lax.bitwise_xor(me, 3)
    barrier = pltpu.get_barrier_semaphore()
    for peer in (xp, diag, sib):
        pl.semaphore_signal(barrier, inc=1, device_id=(peer, b), device_id_type=MESH)
    pairs = ((w_ref, w_v), (c_ref, c_v), (x_ref, x_v), (cot_ref, cot_v), (bias_ref, bias_v), (len_ref, len_v), (gain_ref, gain_v), (shift_ref, shift_v))
    loads = [pltpu.make_async_copy(s, d, lsem.at[n]) for n, (s, d) in enumerate(pairs)]
    for cp in loads:
        cp.start()
    lane = lax.broadcasted_iota(jnp.int32, (XR, 128), 1)
    stage[...] = jnp.zeros((PR, 128), F32)
    cst[...] = jnp.zeros((XR, 128), F32)
    loads[0].wait()
    loads[1].wait()
    stage[:H, :E] = w_v[...].astype(F32)
    cst[:E, :E] = c_v[...].astype(F32)
    for q, p in enumerate(pack(lambda q: stage[q * XR:(q + 1) * XR, :], cst[...], lane)):
        stage[q * XR:(q + 1) * XR, :] = p
    blk[me] = stage[...].astype(BF16)
    pl.semaphore_wait(barrier, 3)
    cuts = ((0, 128), (128, 128), (256, PR - 256))
    def copy(n, slot, r0, nr, peer):
        return pltpu.make_async_remote_copy(src_ref=blk.at[slot, pl.ds(r0, nr)], dst_ref=blk.at[slot, pl.ds(r0, nr)],
            send_sem=ssem.at[n], recv_sem=rsem.at[n], device_id=(peer, b), device_id_type=MESH)
    first = [copy(n, me, r0, nr, xp) for n, (r0, nr) in enumerate(cuts)]
    first.append(copy(3, me, *cuts[2], diag))
    first.append(copy(4, me, 0, PR, sib))
    for cp in first:
        cp.start()
    for cp in loads[2:]:
        cp.wait()
    xpad[...] = jnp.zeros((48, 128), F32)
    def prep(i, _):
        r = pl.ds(pl.multiple_of(i * 48, 48), 48)
        l = lax.broadcasted_iota(jnp.int32, (48, 128), 1)
        xpad[:, :E] = x_v[r, :].astype(F32)
        xs_out[r, :] = jnp.where(l < OFF + E, pltpu.roll(xpad[...], OFF, 1), jnp.where(l < OFF + E + ONES, 1.0, 0.0))
        for k in range(3):
            cotf_out[k, r, :] = cot_v[r, k * 128:(k + 1) * 128].astype(F32)
        cotf_out[3, r, :] = jnp.zeros((48, 128), F32)
        cotf_out[3, r, :OFF] = cot_v[r, LT:].astype(F32)
        return 0
    lax.fori_loop(0, B * T // 48, prep, 0)
    col48 = lax.broadcasted_iota(jnp.int32, (B, B), 1)
    row48 = lax.broadcasted_iota(jnp.int32, (B, B), 0)
    def turn(col):
        return jnp.sum(jnp.where(col48 == row48, jnp.broadcast_to(col, (B, B)), 0.0), 0, keepdims=True)
    ln = jnp.broadcast_to(len_v[...], (B, B)).astype(F32)
    key = ln * 64.0 + (B - 1 - col48).astype(F32)
    kcol = jnp.sum(jnp.where(col48 == row48, key, 0.0), 1, keepdims=True)
    rank = jnp.sum(jnp.where(kcol > key, 1.0, 0.0), 0, keepdims=True)
    hit = jnp.broadcast_to(rank, (B, B)) == row48.astype(F32)
    lcol = jnp.sum(jnp.where(hit, ln, 0.0), 1, keepdims=True)
    lens_out[...] = jnp.broadcast_to(lcol, (B, 128))
    most = jnp.zeros((B, 1), F32)
    row1 = lax.broadcasted_iota(jnp.int32, (B, 1), 0)
    for g, end in enumerate(PLANS[0]):
        most = jnp.where(row1 // SUB == g, float(end), most)
    fits = jnp.where(jnp.max(lcol - most, 0, keepdims=True) > 0.0, 0.0, 1.0)
    info_out[...] = jnp.zeros((SUB, 128), jnp.int32)
    info_out[0:1, :B] = rank.astype(jnp.int32)
    info_out[1:2, :B] = turn(jnp.sum(jnp.where(hit, col48.astype(F32), 0.0), 1, keepdims=True)).astype(jnp.int32)
    info_out[2:3, :B] = jnp.broadcast_to(fits, (1, B)).astype(jnp.int32)
    for src, out in ((gain_v, gain_out), (shift_v, shift_out)):
        out[...] = jnp.zeros((SUB, HP), F32)
        out[:, :H] = jnp.broadcast_to(src[...], (SUB, H))
    brow[...] = jnp.zeros((SUB, HP), F32)
    brow[:1, :H] = bias_v[...]
    passed = []
    for n in range(2):
        first[n].wait_recv()
        cp = copy(5 + n, xp, *cuts[n], sib)
        cp.start()
        passed.append(cp)
    for cp in first[2:] + passed:
        cp.wait_recv()
    for cp in first + passed:
        cp.wait_send()
    bias = brow[:1, :]
    hi = bias.astype(BF16).astype(F32)
    mid = (bias - hi).astype(BF16).astype(F32)
    lo = bias - hi - mid
    def lay(rows, l):
        b0, b1, b2, b3 = rows
        b1, b2, b3 = pltpu.roll(b1, 100, 1), pltpu.roll(b2, 72, 1), pltpu.roll(b3, 44, 1)
        return [jnp.where(l < 100, b0, b1), jnp.where(l < 72, b1, b2), jnp.where(l < 44, b2, b3), jnp.where(l < 16, b3, 0.0)]
    l80 = lax.broadcasted_iota(jnp.int32, (80, 128), 1)
    for r in range(0, H, 80):
        for k, v in enumerate(lay([blk[k, r:r + 80, :].astype(F32) for k in range(4)], l80)):
            wc_out[r:r + 80, k * 128:(k + 1) * 128] = v.astype(BF16)
    for k in range(4):
        stage[...] = blk[k].astype(F32)
        cst4 = unpack_extra(lambda q: stage[q * XR:(q + 1) * XR, :], lane)
        blk[k, :XR + 8, :] = jnp.concatenate([cst4, jnp.zeros((8, 128), F32)], 0).astype(BF16)
    row = lax.broadcasted_iota(jnp.int32, (HP - H, 128), 0)
    l112 = lax.broadcasted_iota(jnp.int32, (HP - H, 128), 1)
    for k, v in enumerate(lay([blk[k, :HP - H, :].astype(F32) for k in range(4)], l112)):
        for n, part in enumerate((hi, mid, lo)):
            v = jnp.where(row == E + n, jnp.broadcast_to(part[:, k * 128:(k + 1) * 128], (HP - H, 128)), v)
        wc_out[H:, k * 128:(k + 1) * 128] = v.astype(BF16)


def gather_call(w, c, bias, lengths, x, cot, gain, shift):
    D = pltpu.SemaphoreType.DMA
    V = pltpu.VMEM
    S = jax.ShapeDtypeStruct
    return pl.pallas_call(
        gather_body,
        out_shape=(S((HP, HP), BF16), S((SUB, 128), jnp.int32), S((B, 128), F32), S((B * T, 128), F32), S((NT, B * T, 128), F32), S((SUB, HP), F32), S((SUB, HP), F32)),
        in_specs=[pl.BlockSpec(memory_space=pltpu.HBM)] * 8,
        scratch_shapes=[V((H, E), BF16), V((E, E), BF16), V((1, H), F32), V((1, B), jnp.int32), V((B * T, E), BF16), V((B * T, H), BF16),
            V((1, H), F32), V((1, H), F32),
            V((4, PR, 128), BF16), V((PR, 128), F32), V((XR, 128), F32), V((SUB, HP), F32), V((48, 128), F32), D((7,)), D((7,)), D((8,))],
        compiler_params=pltpu.CompilerParams(collective_id=0, has_side_effects=True, vmem_limit_bytes=12 * 2**20),
    )(*[pltpu.with_memory_space_constraint(v, pltpu.HBM) for v in (
        w, c, bias.reshape(1, H), lengths.reshape(1, B), x.reshape(B * T, E), cot.reshape(B * T, H), gain.reshape(1, H), shift.reshape(1, H))])


OWN = 4
FIRST = 2


def spans():
    tiles = PR // 16
    return tiles // OWN, tiles % OWN


def reduce_body(nb, hx, dp, sums_ref, out_ref, blk, pk, sib_in, rs_out, rs_in, ssem, srsem, rsem_s, rsem_r, asem_s, asem_r):
    me, b = lax.axis_index("tm"), lax.axis_index("batch")
    core, sib, xi = lax.rem(me, 2), lax.bitwise_xor(me, 1), me // 2
    group = b // nb * nb
    rank = b - group
    base, more = spans()
    big, small = (base + 1) * 16, base * 16
    barrier = pltpu.get_barrier_semaphore()
    pl.semaphore_signal(barrier, inc=1, device_id=(sib, b), device_id_type=MESH)
    others = [(dx, db) for db in range(nb) for dx in range(2) if dx or db]
    for dx, db in others:
        pl.semaphore_signal(barrier, inc=1, device_id=(2 * lax.rem(xi + dx, 2) + core, group + lax.rem(rank + db, nb)), device_id_type=MESH)
    def blocks(t, l):
        t0, t1, t2, t3 = t
        return [t0,
            jnp.where(l < 28, pltpu.roll(t0, 28, 1), pltpu.roll(t1, 28, 1)),
            jnp.where(l < 56, pltpu.roll(t1, 56, 1), pltpu.roll(t2, 56, 1)),
            jnp.where(l < 84, pltpu.roll(t2, 84, 1), pltpu.roll(t3, 84, 1))]
    gsum = jnp.sum(sums_ref[:SUB, :], 0, keepdims=True)
    ssum = jnp.sum(sums_ref[SUB:, :], 0, keepdims=True)
    l128 = lax.broadcasted_iota(jnp.int32, (128, 128), 1)
    r128 = lax.broadcasted_iota(jnp.int32, (128, 128), 0)
    for m in range(4):
        prod = lax.dot_general(hx[:, m * 128:(m + 1) * 128], dp[...], (((0,), (0,)), ((), ())), preferred_element_type=F32)
        t = [prod[:, k * 128:(k + 1) * 128] for k in range(4)]
        if m == 3:
            for k in range(4):
                gk = jnp.broadcast_to(gsum[:, k * 128:(k + 1) * 128], (128, 128))
                sk = jnp.broadcast_to(ssum[:, k * 128:(k + 1) * 128], (128, 128))
                t[k] = jnp.where(r128 == OFF + E + 1, gk, jnp.where(r128 == OFF + E + 2, sk, t[k]))
        for k, v in enumerate(blocks(t, l128)):
            blk[k, m * 128:(m + 1) * 128, :] = v
    lane = lax.broadcasted_iota(jnp.int32, (XR, 128), 1)
    for k in range(4):
        extra = blk[k, H:H + XR, :]
        blk[k, H:H + 16, :] = jnp.zeros((16, 128), F32)
        for q, p in enumerate(pack(lambda q: blk[k, q * XR:(q + 1) * XR, :], extra, lane)):
            blk[k, q * XR:(q + 1) * XR, :] = p
        pk[k] = blk[k, :PR, :].astype(BF16)
    pl.semaphore_wait(barrier, len(others) + 1)
    scopies = []
    for j in range(2):
        cp = pltpu.make_async_remote_copy(src_ref=pk.at[2 * j + (1 - core)], dst_ref=sib_in.at[j], send_sem=ssem.at[j], recv_sem=srsem.at[j],
            device_id=(sib, b), device_id_type=MESH)
        cp.start()
        scopies.append(cp)
    def sized(owner, run):
        pl.when(owner < more)(lambda: run(big))
        pl.when(owner >= more)(lambda: run(small))
    def span(owner, rows):
        return pl.ds(pl.multiple_of((owner * base + lax.min(owner, more)) * 16, 16), rows)
    mine = xi * nb + rank
    owner = rank - FIRST
    is_owner = (owner >= 0) & (owner < OWN)
    far = 2 - 2 * (rank // (nb // 2))
    def rcopy(px, o, rows):
        n = px * OWN + o
        return pltpu.make_async_remote_copy(src_ref=rs_out.at[px, span(o, rows)], dst_ref=rs_in.at[mine, pl.ds(0, rows)],
            send_sem=rsem_s.at[n], recv_sem=rsem_r.at[mine], device_id=(2 * px + core, group + FIRST + o), device_id_type=MESH)
    def arrived(slot, rows):
        return pltpu.make_async_remote_copy(src_ref=rs_out.at[0, pl.ds(0, rows)], dst_ref=rs_in.at[slot, pl.ds(0, rows)],
            send_sem=rsem_s.at[0], recv_sem=rsem_r.at[slot], device_id=(2 * (1 - xi) + core, b), device_id_type=MESH)
    def targets():
        for px in range(2):
            for n in range(OWN):
                o = lax.rem(far + n, OWN)
                yield px, o, (px != xi) | (o != owner)
    def acopy(db, o, rows):
        return pltpu.make_async_remote_copy(src_ref=out_ref.at[span(o, rows)], dst_ref=out_ref.at[span(o, rows)], send_sem=asem_s.at[db],
            recv_sem=asem_r.at[o], device_id=(me, group + lax.rem(rank + db, nb)), device_id_type=MESH)
    for j in range(2):
        scopies[j].wait_recv()
        rs_out[j] = (blk[2 * j + core, :PR, :] + sib_in[j].astype(F32)).astype(BF16)
        for px, o, other in targets():
            if px == j:
                pl.when(other)(lambda px=px, o=o: sized(o, lambda rows: rcopy(px, o, rows).start()))
    def collect(rows):
        total = rs_out[xi, span(owner, rows), :].astype(F32)
        for n in range(1, 2 * nb):
            slot = lax.rem(mine + n, 2 * nb)
            arrived(slot, rows).wait_recv()
            total = total + rs_in[slot, :rows, :].astype(F32)
        out_ref[span(owner, rows), :] = total.astype(BF16)
        for db in range(1, nb):
            acopy(db, owner, rows).start()
    pl.when(is_owner)(lambda: sized(owner, collect))
    for o in range(OWN):
        rows = big if o < more else small
        pl.when(owner != o)(lambda o=o, rows=rows: acopy(1, o, rows).wait_recv())
    for cp in scopies:
        cp.wait_send()
    for px, o, other in targets():
        pl.when(other)(lambda px=px, o=o: sized(o, lambda rows: rcopy(px, o, rows).wait_send()))
    def sent(rows):
        for db in range(1, nb):
            acopy(db, owner, rows).wait_send()
    pl.when(is_owner)(lambda: sized(owner, sent))


def reduce_call(hx, dp, sums, nb):
    D = pltpu.SemaphoreType.DMA
    V = pltpu.VMEM
    vs = pl.BlockSpec(memory_space=pltpu.VMEM)
    big = (spans()[0] + 1) * 16
    return pl.pallas_call(
        functools.partial(reduce_body, nb),
        out_shape=jax.ShapeDtypeStruct((PR, 128), BF16),
        in_specs=[vs, vs, vs],
        out_specs=vs,
        scratch_shapes=[V((4, HP, 128), F32), V((4, PR, 128), BF16), V((2, PR, 128), BF16),
            V((2, PR, 128), BF16), V((2 * nb, big, 128), BF16),
            D((2,)), D((2,)), D((2 * OWN,)), D((2 * nb,)), D((nb,)), D((OWN,))],
        compiler_params=pltpu.CompilerParams(collective_id=1, has_side_effects=True, vmem_limit_bytes=16 * 2**20),
    )(hx, dp, sums)


def spread_body(p_ref, gw_out, gc_out, gb_out, gg_out, gs_out, stage):
    stage[...] = p_ref[...].astype(F32)
    gw_out[...] = stage[:H, :E]
    lane = lax.broadcasted_iota(jnp.int32, (XR, 128), 1)
    extra = unpack_extra(lambda q: stage[q * XR:(q + 1) * XR, :], lane)
    stage[:XR, :] = extra
    gc_out[...] = stage[:E, :E]
    for n, ref in enumerate((gb_out, gg_out, gs_out)):
        ref[...] = stage[E + n:E + n + 1, :E]


def spread_call(p):
    S = jax.ShapeDtypeStruct
    vec = S((1, E), F32)
    return pl.pallas_call(
        spread_body,
        out_shape=(S((H, E), F32), S((E, E), F32), vec, vec, vec),
        scratch_shapes=[pltpu.VMEM((PR, 128), F32)],
        compiler_params=pltpu.CompilerParams(vmem_limit_bytes=8 * 2**20),
    )(p)


def per_device(inputs, lengths, w_rec, w_in, rec_bias, norm_gain, norm_shift, cotangent, nb):
    wc, info, lens, xs, cotf, gain, shift = gather_call(w_rec, w_in, rec_bias, lengths, inputs, cotangent, norm_gain, norm_shift)
    hid, gx, hx, dp, sums = cell_call(info, xs, lens, cotf, wc, gain, shift)
    group = math.gcd(nb, 8)
    p = reduce_call(hx, dp, sums, group)
    if nb > group:
        p = lax.all_gather(p.astype(F32), "batch").reshape(nb // group, group, PR, 128)[:, 0].sum(0)
    gw, gc, gb, gg, gs = spread_call(p)
    return hid.reshape(B, T, H), gx.reshape(B, T, E), gw, gc, gb.reshape(E), gg.reshape(E), gs.reshape(E)


def solution(mesh):
    both = ("tm", "batch")
    return jax.shard_map(
        functools.partial(per_device, nb=mesh.shape["batch"]),
        mesh=mesh,
        in_specs=(P(both, None, None), P(both), P(None, "tm"), P(None, "tm"), P(), P(), P(), P(both, None, None)),
        out_specs=(P(both, None, None), P(both, None, None), P(None, "tm"), P(None, "tm"), P("tm"), P("tm"), P("tm")),
        check_vma=False,
    )
```

time: 894 us -> 45.6 us (0.05); the launches traced: 881 us -> 45.4 us
  matrix products: 538 us -> 0 us
  other arithmetic: 133 us -> 0 us
  waiting for transfers between devices: 66 us -> 0 us
  local copies, waits for them, and re-layouts: 55 us -> 0 us
  blocking collectives: 54.4 us -> 0 us
  Pallas kernels: 0 us -> 44.8 us
  between operations: 34.3 us -> 0.65 us
    dot_general x645 -> x0, matrix products: 538 us -> none  [the longest x46 63.8 us: run_block(): jnp.einsum('bih,bh->bi', earlier, first_act, precision=EXACT) * decays]
    reduce_sum x184 -> x0, other arithmetic: 68.5 us -> none  [the longest x46 37.7 us: back_block(): bias_sum = bias_sum + jnp.sum(d_pre.astype(jnp.float32), 0)]
    psum x1 -> x0, waiting for transfers between devices: 65.9 us -> none  [per_device(): lax.psum((sums[0], sums[1], sums[2], sums[3], sums[4]), ('tm', 'batch'))]
    pallas_call x0 -> x4, Pallas kernels: none -> 44.8 us  [the longest x1 18.5 us: cell_call(): pl.pallas_call(cell_body, out_shape=(S((B * T, H), BF16), S((B * T, E), F...]
    unnamed x2276 -> x0, local copies, waits for them, and re-layouts: 41.3 us -> none
    psum x1 -> x0, blocking collectives: 40.8 us -> none  [per_device(): lax.psum((sums[0], sums[1], sums[2], sums[3], sums[4]), ('tm', 'batch'))]
    unnamed x472 -> x0, other arithmetic: 34.2 us -> none
    all_gather x2 -> x0, blocking collectives: 13.6 us -> none  [the longest x1 7.22 us: per_device(): lax.all_gather(w_rec, 'tm', axis=1, tiled=True)]
where the time goes in v2:
time: 45.6 us; the launch traced here: 45.4 us
  Pallas kernels  44.8 us (98%)
  between operations  0.65 us (1%)
    pallas_call x1, Pallas kernels, cell_call(): pl.pallas_call(cell_body, out_shape=(S((B * T, H), BF16), S((B * T, E), F...  18.5 us
    pallas_call x1, Pallas kernels, reduce_call(): pl.pallas_call(functools.partial(reduce_body, nb), out_shape=jax.ShapeDty...  17.2 us
    pallas_call x1, Pallas kernels, gather_call(): pl.pallas_call(gather_body, out_shape=(S((HP, HP), BF16), S((SUB, 128), j...  8.35 us

profile of v2, /device:TPU:0, one launch (start us, length us, event | category | flops | bytes accessed | tf_op | source)
XLA Modules:
  0.0 45.4 jit_solution(6374511165121357466)
XLA Ops:
  0.6 8.4 %shard_map.135 = (bf16[512,512]{1,0:T(8,128)(2,1)S(1)}, s32[8,128]{1,0:T(8,128)S(1)}, f32[48,128]{1,0:T(8,128)S(1)}, f32[1152,128]{1,0:T(8,128)S(1)}, f32[4,1152...) custom-call(bf16[400,100]{1,0:T(8,128)(2,1)} %w_ref.1, bf16[100,100]{1,0:T(8,128)(2,1)} %c_ref.1, ...), custom_call_target="tpu_custom_call" | custom-call | tf_op jit(solution)/shard_map/pallas_call | solution.py:400
  9.0 18.5 %shard_map.136 = (bf16[1152,400]{1,0:T(8,128)(2,1)}, f32[1152,100]{1,0:T(8,128)}, bf16[1008,512]{1,0:T(8,128)(2,1)S(1)}, bf16[1008,512]{1,0:T(8,128)(2,1)S(1)}, f32[16,512]{1,0:T(8,128)S(1)}) custom-call(s32[8,128]{1,0:T(8,128)S(1)} %get-tuple-element.24.info, f32[1152,128]{1,0:T(8,128)S(1)} %get-tuple-element.25.xs_in, ...), custom_call_target="tpu_custom_call" | custom-call | tf_op jit(solution)/shard_map/pallas_call | solution.py:256
  27.5 17.2 %shard_map.137.p_ref = bf16[416,128]{1,0:T(8,128)(2,1)S(1)} custom-call(bf16[1008,512]{1,0:T(8,128)(2,1)S(1)} %get-tuple-element.33.hx, bf16[1008,512]{1,0:T(8,128)(2,1)S(1)} %get-tuple-element.34.dp, f32[16,512]{1,0:T(8,128)S(1)} %get-tuple-element.35.sums_ref), custom_call_target="tpu_custom_call" | custom-call | tf_op jit(solution)/shard_map/pallas_call | solution.py:525
  44.7 0.7 %shard_map.138 = (f32[400,100]{1,0:T(8,128)}, f32[100,100]{1,0:T(8,128)}, f32[1,100]{1,0:T(1,128)}, f32[1,100]{1,0:T(1,128)}, f32[1,100]{1,0:T(1,128)}) custom-call(bf16[416,128]{1,0:T(8,128)(2,1)S(1)} %shard_map.137.p_ref), custom_call_target="tpu_custom_call" | custom-call | tf_op jit(solution)/shard_map/pallas_call | solution.py:551

commit v3 on v2

--- a/solution.py
+++ b/solution.py
@@ -27,25 +27,27 @@
 PLANS = ((21, 21, 19, 17, 14, 11), (TV,) * (B // SUB))
 
 
-def cell_body(info, xs_in, lens_ref, cotf_in, wc_ref, gain_p, shift_p, hid_out, gx_out, hx, dpre_s, sums_out, xs, cotf, gxs, hidf, h_s, *rest):
+def cell_body(info, xs_in, lens_ref, cotf_in, wc_ref, gain_p, shift_p, hid_out, gx_out, hx, dpre_s, sums_out, hid_v, sem, xs, cotf, gxs, hidf, h_s, *rest):
     accs = [pltpu.ACC(m)((ROWS, 256), F32) for _ in range(NC) for m in range(2)]
     def place(row, n):
         return pl.ds(pl.multiple_of(info[row, n] * T, SUB), T)
     for r in range(B):
         xs[r * T:(r + 1) * T, :] = xs_in[place(1, r), :]
+    hid_copy = pltpu.make_async_copy(hid_v, hid_out, sem)
     h_s[...] = jnp.zeros((B, HP), F32)
     sums_out[...] = jnp.zeros((2 * SUB, HP), F32)
     def scoped(*a):
         def run(ends):
-            cell_inner(ends, place, xs, lens_ref, cotf_in, wc_ref, gain_p, shift_p, hid_out, hx, dpre_s, sums_out,
+            cell_inner(info[2, 0] >= 0, ends, place, xs, lens_ref, cotf_in, wc_ref, gain_p, shift_p, hid_v, hx, dpre_s, sums_out, hid_copy,
                 cotf, gxs, hidf, h_s, *rest, [a[2 * i:2 * i + 2] for i in range(NC)])
         lax.cond(info[2, 0] > 0, lambda: run(PLANS[0]), lambda: run(PLANS[1]))
     pl.run_scoped(scoped, *accs)
     for b in range(B):
         gx_out[b * T:(b + 1) * T, :] = gxs[place(0, b), :E]
-
-
-def cell_inner(ends, place, xs, lens_ref, cotf_in, wc_ref, gain_p, shift_p, hid_out, hx, dpre_s, sums_out,
+    hid_copy.wait()
+
+
+def cell_inner(go, ends, place, xs, lens_ref, cotf_in, wc_ref, gain_p, shift_p, hid_out, hx, dpre_s, sums_out, hid_copy,
         cotf, gxs, hidf, h_s, grad_s, first_s, slope_s, s_s, xh_s, rstd_s, pt_s, pc_s, f_s, mt_s, dmix_s, accs):
     lane = lax.broadcasted_iota(jnp.int32, (SUB, 128), 1)
     lane16 = lax.broadcasted_iota(jnp.int32, (ROWS, 128), 1)
@@ -228,20 +230,20 @@
             sums_out[:SUB, cut(k)] += sums[0][k]
             sums_out[SUB:, cut(k)] += sums[1][k]
 
-    todo = list(range(B))
+    def fwd_part(t):
+        fwd_step(t)
+        for r in range(-(-B * t // TV), -(-B * (t + 1) // TV)):
+            sort_cot(r)
+    def bwd_part(t):
+        bwd_step(t)
+        for i in range(2 * (TV - 1 - t), min(2 * (TV - t), B // 2)):
+            fin(i)
     for t in range(TV):
-        fwd_step(t)
-        n = -(-len(todo) // (TV - t))
-        for r in todo[:n]:
-            sort_cot(r)
-        todo = todo[n:]
-    todo = list(range(B // 2))
+        pl.when(go)(lambda t=t: fwd_part(t))
     for t in range(TV - 1, -1, -1):
-        bwd_step(t)
-        n = -(-len(todo) // (t + 1))
-        for i in todo[:n]:
-            fin(i)
-        todo = todo[n:]
+        pl.when(go)(lambda t=t: bwd_part(t))
+        if t == TV - B // 4:
+            hid_copy.start()
     for t in range(TV, T):
         gxs[pl.ds(t, B, stride=T), :] = jnp.zeros((B, 128), F32)
 
@@ -255,9 +257,10 @@
     vs = pl.BlockSpec(memory_space=pltpu.VMEM)
     return pl.pallas_call(
         cell_body,
+        out_specs=[pl.BlockSpec(memory_space=pl.ANY)] + [vs] * 4,
         out_shape=(S((B * T, H), BF16), S((B * T, E), F32), S((TV * B, HP), BF16), S((TV * B, HP), BF16), S((2 * SUB, HP), F32)),
         in_specs=[pl.BlockSpec(memory_space=pltpu.SMEM)] + [vs] * 6,
-        scratch_shapes=[seq, wide, seq, wide, V((B, HP), F32), V((B, HP), F32),
+        scratch_shapes=[V((B * T, H), BF16), pltpu.SemaphoreType.DMA, seq, wide, seq, wide, V((B, HP), F32), V((B, HP), F32),
             big, big, big, big, V((TV, B, 128), F32), big, big, pair, pair, big],
         compiler_params=pltpu.CompilerParams(vmem_limit_bytes=44 * 2**20),
     )(info, xs, lens, cotf, wc, gain_p, shift_p)

time: 45.6 us -> 45.8 us (level)
  no operation moved by 1% of the time
where the time goes in v3:
time: 45.8 us; the launch traced here: 45.6 us
  Pallas kernels  45 us (98%)
  between operations  0.66 us (1%)
    pallas_call x1, Pallas kernels, cell_call(): pl.pallas_call(cell_body, out_specs=[pl.BlockSpec(memory_space=pl.ANY)] +...  18.5 us
    pallas_call x1, Pallas kernels, reduce_call(): pl.pallas_call(functools.partial(reduce_body, nb), out_shape=jax.ShapeDty...  17.3 us
    pallas_call x1, Pallas kernels, gather_call(): pl.pallas_call(gather_body, out_shape=(S((HP, HP), BF16), S((SUB, 128), j...  8.35 us

profile of v3, /device:TPU:0, one launch (start us, length us, event | category | flops | bytes accessed | tf_op | source)
XLA Modules:
  0.0 45.6 jit_solution(3234592236038713417)
XLA Ops:
  0.6 8.4 %shard_map.135 = (bf16[512,512]{1,0:T(8,128)(2,1)S(1)}, s32[8,128]{1,0:T(8,128)S(1)}, f32[48,128]{1,0:T(8,128)S(1)}, f32[1152,128]{1,0:T(8,128)S(1)}, f32[4,1152...) custom-call(bf16[400,100]{1,0:T(8,128)(2,1)} %w_ref.1, bf16[100,100]{1,0:T(8,128)(2,1)} %c_ref.1, ...), custom_call_target="tpu_custom_call" | custom-call | tf_op jit(solution)/shard_map/pallas_call | solution.py:403
  9.0 18.5 %shard_map.136 = (bf16[1152,400]{1,0:T(8,128)(2,1)}, f32[1152,100]{1,0:T(8,128)}, bf16[1008,512]{1,0:T(8,128)(2,1)S(1)}, bf16[1008,512]{1,0:T(8,128)(2,1)S(1)}, f32[16,512]{1,0:T(8,128)S(1)}) custom-call(s32[8,128]{1,0:T(8,128)S(1)} %get-tuple-element.24.info, f32[1152,128]{1,0:T(8,128)S(1)} %get-tuple-element.25.xs_in, ...), custom_call_target="tpu_custom_call" | custom-call | tf_op jit(solution)/shard_map/pallas_call | solution.py:258
  27.5 17.3 %shard_map.137.p_ref = bf16[416,128]{1,0:T(8,128)(2,1)S(1)} custom-call(bf16[1008,512]{1,0:T(8,128)(2,1)S(1)} %get-tuple-element.33.hx, bf16[1008,512]{1,0:T(8,128)(2,1)S(1)} %get-tuple-element.34.dp, f32[16,512]{1,0:T(8,128)S(1)} %get-tuple-element.35.sums_ref), custom_call_target="tpu_custom_call" | custom-call | tf_op jit(solution)/shard_map/pallas_call | solution.py:528
  44.9 0.7 %shard_map.138 = (f32[400,100]{1,0:T(8,128)}, f32[100,100]{1,0:T(8,128)}, f32[1,100]{1,0:T(1,128)}, f32[1,100]{1,0:T(1,128)}, f32[1,100]{1,0:T(1,128)}) custom-call(bf16[416,128]{1,0:T(8,128)(2,1)S(1)} %shard_map.137.p_ref), custom_call_target="tpu_custom_call" | custom-call | tf_op jit(solution)/shard_map/pallas_call | solution.py:554
